TPU v7x, 32 devices: a whole 2x2x4 slice. The times are simulated.
32 devices in a mesh: dp: 4 (over y, core), cell: 8 (over z, x).
Axes of the slice: x: 2, y: 2, z: 4, core: 2. Of those that a mesh axis runs over, the one named last changes fastest.
Arguments:
- sensitivity: bfloat16 [512, 50176], P('dp', 'cell'), may hold values from -0.078125 to 0.078125
- direction: bfloat16 [16, 50176], P(None, 'cell'), may hold values from -6 to 6
- depth_weight: float32 [50176], P('cell'), may hold values from 0.3 to 3
- counts: int32 [8], P('cell'), may hold values from 4704 to 6272, as said below
- send_lists: int32 [8, 2, 128], P('cell'), may hold values from 0 to 6271, as said below
- neighbours: int32 [6, 50176], P(None, 'cell'), may hold values from 0 to 6528, as said below
Outputs:
- product: float32 [16, 50176], P(None, 'cell')
Inputs may be any that keep to these rules, and one draw needn't show every extreme that they name: `counts`: every partition has at least 4704 live cells; some partition is full in every draw. `send_lists`: entries are local indices of live cells of their own partition. `neighbours`: entries below 6272 are live local cells that differ from the cell's own local index by at most 64; 6272 to 6527 name received rim cells; 6528 is an absent face; padded slots hold only absent faces.
All inputs are finite; a program needn't handle non-finite values.
Results may differ from a plain program's by a relative error of at most 0.0008.
Values sent between devices are 32-bit elements; how exact they have to be, the bound alone decides.
A program may use at most 64 MiB of HBM per device.

v0:
```python
import jax
import jax.numpy as jnp
from jax import lax
from jax.sharding import PartitionSpec as P


def padded_2(value, sides, width):
    for axis, dim in sides:
        count, length = (lax.axis_size(axis), value.shape[dim])
        up = [(i, (i + 1) % count) for i in range(count - 1)]
        down = [(j, i) for i, j in up]
        last = lax.slice_in_dim(value, length - width, length, axis=dim)
        leading = lax.slice_in_dim(value, 0, width, axis=dim)
        before = lax.ppermute(last, axis, up)
        after = lax.ppermute(leading, axis, down)
        value = jnp.concatenate([before, value, after], axis=dim)
    return value


def pick_block(width):
    block_len = 8
    for candidate in range(128, 7, -8):
        if width % candidate == 0:
            block_len = candidate
            break
    return block_len


def pick_group(block_count):
    group_len = 1
    for candidate in range(1, 9):
        if block_count % candidate == 0:
            group_len = candidate
    return group_len


def smoothness(masked_f, weight, send_lists, neighbours, start, width):
    slots = masked_f.shape[1]
    values = jnp.concatenate([masked_f * weight[None, :], weight[None, :]], axis=0)
    picked = jnp.take(values, send_lists[0].reshape(-1), axis=1)
    rim = picked.shape[1] // 2
    padded = padded_2(picked, (("cell", 1),), rim)
    rim_vals = jnp.concatenate([padded[:, :rim], padded[:, 3 * rim :]], axis=1)
    lanes = values.shape[0]
    block_len = pick_block(width)
    block_count = width // block_len
    pieces = 1 + (128 + block_len - 1) // block_len
    spread = jnp.pad(values, ((0, 0), (64, pieces * block_len)))
    local_vals = lax.dynamic_slice_in_dim(spread, start, (block_count + pieces - 1) * block_len, 1)
    shifted = [
        local_vals[:, m * block_len : (m + block_count) * block_len].reshape(
            lanes, block_count, block_len
        )
        for m in range(pieces)
    ]
    rim_part = jnp.broadcast_to(rim_vals[:, None, :], (lanes, block_count, 2 * rim))
    windows = jnp.concatenate(shifted + [rim_part], axis=2).transpose(1, 0, 2)
    span = windows.shape[2]
    faces = lax.dynamic_slice_in_dim(neighbours, start, width, 1)
    position = jnp.arange(width, dtype=jnp.int32)
    anchor = start + position // block_len * block_len
    column = jnp.where(
        faces < slots,
        faces - anchor[None, :] + 64,
        jnp.where(faces < slots + 2 * rim, pieces * block_len + faces - slots, -1),
    )
    column = column.reshape(faces.shape[0], block_count, block_len).transpose(1, 0, 2)
    group_len = pick_group(block_count)
    windows = windows.reshape(block_count // group_len, group_len, lanes, span)
    column = column.reshape(block_count // group_len, group_len, faces.shape[0], block_len)

    def gather_block(item):
        window_set, column_set = item
        target = jnp.arange(span, dtype=jnp.int32)[None, None, :, None]
        hits = jnp.sum((column_set[:, :, None, :] == target).astype(jnp.float32), axis=1)
        return jnp.einsum("grw,gwb->grb", window_set, hits, precision=lax.Precision.HIGHEST)

    sums = lax.map(gather_block, (windows, column))
    sums = sums.reshape(block_count, lanes, block_len).transpose(1, 0, 2).reshape(lanes, width)
    own_p = lax.dynamic_slice_in_dim(masked_f, start, width, 1)
    own_w = lax.dynamic_slice_in_dim(weight, start, width, 0)
    coupling = own_p * sums[-1][None, :] - sums[:-1]
    return own_w[None] * own_w[None] * own_p + own_w[None] * coupling


def on_device(sensitivity, direction, depth_weight, counts, send_lists, neighbours):
    slots = sensitivity.shape[1]
    nvecs = direction.shape[0]
    live = jnp.arange(slots, dtype=jnp.int32) < counts[0]
    masked = jnp.where(live[None, :], direction, jnp.zeros_like(direction))
    partial_data = lax.dot_general(
        masked, sensitivity, (((1,), (1,)), ((), ())), preferred_element_type=jnp.float32
    )
    summed = lax.psum(partial_data, "cell")
    rounded = summed.astype(jnp.bfloat16)
    remainder = (summed - rounded.astype(jnp.float32)).astype(jnp.bfloat16)
    stacked = jnp.concatenate([rounded, remainder], axis=0)
    both = jnp.dot(stacked, sensitivity, preferred_element_type=jnp.float32)
    partial_cells = both[:nvecs] + both[nvecs:]
    weight = jnp.where(live, depth_weight, jnp.float32(0.0))
    masked_f = masked.astype(jnp.float32)
    misfit = lax.psum_scatter(partial_cells, "dp", scatter_dimension=1, tiled=True)
    width = misfit.shape[1]
    start = lax.axis_index("dp") * width
    smooth = smoothness(masked_f, weight, send_lists, neighbours, start, width)
    live_share = lax.dynamic_slice_in_dim(live, start, width, 0)
    total = jnp.where(live_share[None, :], misfit + 0.5 * smooth, jnp.float32(0.0))
    return lax.all_gather(total, "dp", axis=1, tiled=True)


def solution(mesh):
    placed = (
        P("dp", "cell"),
        P(None, "cell"),
        P("cell"),
        P("cell"),
        P("cell", None, None),
        P(None, "cell"),
    )
    return jax.shard_map(
        on_device, mesh=mesh, in_specs=placed, out_specs=P(None, "cell"), check_vma=False
    )
```

profile of v0, /device:TPU:0, one launch (start us, length us, event | category | flops | bytes accessed | tf_op | source)
XLA Modules:
  0.0 87.3 jit_solution(419671326507697204)
XLA Ops:
  7.3 0.6 copy-done
  8.0 1.4 %fusion.5 = f32[16,128]{1,0:T(8,128)S(1)} fusion(bf16[128,6272]{1,0:T(8,128)(2,1)S(1)} %copy-done, bf16[16,6272]{1,0:T(8,128)(2,1)} %param.9, pred[6272]{0:T(1024)(128)(4,1)S(1)} %iota_compare_fusion.1), kind=kOutput, calls=%fused_computation.18 | convolution fusion | flops 25790464 | bytes 1820800 | tf_op jit(solution)/shard_map/dot_general | solution.py:91
  9.4 23.4 %psum.7 = f32[16,128]{1,0:T(8,128)S(1)} all-reduce(f32[16,128]{1,0:T(8,128)S(1)} %fusion.5), channel_id=1, replica_groups=mesh['dp'=4,'cell'=8] {'cell'}, use_global_device_ids=true, to_apply=%region_0.1 | all-reduce | flops 2048 | bytes 16384 | tf_op jit(solution)/shard_map/psum | solution.py:94
  32.8 0.4 fusion.11
  33.2 2.5 %copy.65 = f32[16,6272]{0,1:T(8,128)} copy(f32[16,6272]{1,0:T(8,128)S(1)} %slice_add_fusion) | data formatting | bytes 802816
  35.7 0.7 copy-done.4
  36.5 0.2 copy-done.1
  36.8 2.4 %copy.56 = f32[17,6272]{0,1:T(8,128)} copy(f32[17,6272]{1,0:T(8,128)S(1)} %pad_maximum_fusion.1) | data formatting | bytes 852992 | tf_op jit(solution)/shard_map/concatenate | solution.py:39
  39.2 2.9 %gather_fusion = f32[256,17]{1,0:T(8,128)S(1)} fusion(f32[17,6272]{0,1:T(8,128)} %copy.56, s32[1024]{0:T(1024)S(1)} %pad_clamp_fusion), kind=kCustom, calls=%fused_computation | custom fusion | bytes 35840 | tf_op jit(solution)/shard_map/jit(_take)/gather | solution.py:40
  42.2 0.6 fusion.19
  42.9 1.3 %collective-permute-start.1 = (f32[17,128]{0,1:T(8,128)}, f32[17,128]{0,1:T(8,128)}, u32[]{:S(2)}, u32[]{:S(2)}) collective-permute-start(f32[17,128]{0,1:T(8,128)} %get-tuple-element.44), channel_id=1, source_target_pairs={{1,0},{2,1},{3,2},{4,3},{5,4},{6,5},{7,6},{9,8},{10,9},{11,10},{12... | collective-permute-start | bytes 26120 | tf_op jit(solution)/shard_map/ppermute | solution.py:15
  44.1 4.5 %collective-permute-start = (f32[17,128]{0,1:T(8,128)}, f32[17,128]{0,1:T(8,128)S(1)}, u32[]{:S(2)}, u32[]{:S(2)}) collective-permute-start(f32[17,128]{0,1:T(8,128)} %get-tuple-element.43), channel_id=1, source_target_pairs={{0,1},{1,2},{2,3},{3,4},{4,5},{5,6},{6,7},{8,9},{9,10},{10,11},{11... | collective-permute-start | bytes 26120 | tf_op jit(solution)/shard_map/ppermute | solution.py:14
  48.8 0.2 pad_dynamic-slice_fusion.1
  49.0 0.9 %select_select_fusion = s32[6,1568]{1,0:T(8,128)S(1)} fusion(s32[6,6272]{1,0:T(8,128)} %param.13, s32[]{:T(128)S(6)} %select_n.58, s32[1568]{0:T(1024)S(1)} %fusion.8), kind=kLoop, calls=%fused_computation.23 | loop fusion | flops 65856 | bytes 81540 | tf_op jit(solution)/shard_map/jit(_where)/select_n | solution.py:62
  50.1 0.1 reshape.88
  50.3 0.1 reshape.87
  50.7 0.9 %copy.58 = f32[17,128]{1,0:T(8,128)S(1)} copy(f32[17,128]{0,1:T(8,128)} %collective-permute-done.1) | data formatting | bytes 17408 | tf_op jit(solution)/shard_map/ppermute | solution.py:15
  51.8 0.4 pad_maximum_fusion
  52.2 9.5 %while.10 = (s32[]{:T(128)}, f32[2,7,17,112]{3,2,1,0:T(8,128)}, f32[2,7,17,592]{3,2,1,0:T(8,128)S(1)}, s32[2,7,6,112]{3,2,1,0:T(8,128)S(1)}, s32[]{:T(128)}) while((s32[]{:T(128)}, f32[2,7,17,112]{3,2,1,0:T(8,128)}, f32[2,7,17,592]{3,2,1,0:T(8,128)S(1)}, s32[2,7,6,112]{3,2,1,0:T(8,128)S(1)}, s32[]{:T(128)}) %tuple.29), condition=%wide.region_4.5_spmd, body=%wide.region_2.4_spmd.sunk | while | flops 102572288 | bytes 5290241 | solution.py:78
  52.2 1.9 %convert_reduce_fusion.2 = f32[7,592,112]{1,2,0:T(8,128)S(1)} fusion(s32[7,6,112]{2,1,0:T(8,128)S(1)} %dynamic-slice_bitcast_fusion.2), kind=kLoop, calls=%fused_computation.1.clone.1 | loop fusion | flops 7890176 | bytes 1875328 | tf_op jit(solution)/shard_map/while/body/eval_jaxpr/reduce_sum | solution.py:75
  54.2 2.1 %fusion.28 = f32[2,7,17,112]{3,2,1,0:T(8,128)S(1)} fusion(f32[2,7,17,112]{3,2,1,0:T(8,128)S(1)} %copy-done.2, s32[]{:T(128)S(6)} %copy.72, f32[7,592,112]{1,2,0:T(8,128)S(1)} %convert_reduce_fusion.2, f32[2,7,17,592]{3,2,1,0:T(8,128)S(1)} %get-tuple-element.82), kind=kOutput, calls=%fused_computation.4.clone.1 | convolution fusion | flops 94682112 | bytes 2524160 | tf_op jit(solution)/shard_map/while/body/eval_jaxpr/grw,gwb->grb/dot_general | solution.py:76
  56.3 0.7 copy-done.3
  57.0 1.9 %convert_reduce_fusion.2 = f32[7,592,112]{1,2,0:T(8,128)S(1)} fusion(s32[7,6,112]{2,1,0:T(8,128)S(1)} %dynamic-slice_bitcast_fusion.2), kind=kLoop, calls=%fused_computation.1.clone.1 | loop fusion | flops 7890176 | bytes 1875328 | tf_op jit(solution)/shard_map/while/body/eval_jaxpr/reduce_sum | solution.py:75
  58.9 2.1 %fusion.28 = f32[2,7,17,112]{3,2,1,0:T(8,128)S(1)} fusion(f32[2,7,17,112]{3,2,1,0:T(8,128)S(1)} %copy-done.2, s32[]{:T(128)S(6)} %copy.72, f32[7,592,112]{1,2,0:T(8,128)S(1)} %convert_reduce_fusion.2, f32[2,7,17,592]{3,2,1,0:T(8,128)S(1)} %get-tuple-element.82), kind=kOutput, calls=%fused_computation.4.clone.1 | convolution fusion | flops 94682112 | bytes 2524160 | tf_op jit(solution)/shard_map/while/body/eval_jaxpr/grw,gwb->grb/dot_general | solution.py:76
  61.0 0.7 copy-done.3
  61.7 0.9 %copy.68 = f32[14,17,112]{2,0,1:T(8,128)S(1)} copy(f32[14,17,112]{2,1,0:T(8,128)} %bitcast.54) | data formatting | bytes 213248 | tf_op jit(solution)/shard_map/reshape | solution.py:79
  62.8 8.7 %reduce-scatter.4.cloned.1.call-done = f32[1568,16]{1,0:T(8,128)} async-done(((f32[6272,16]{1,0:T(8,128)}), f32[1568,16]{1,0:T(8,128)}) %reduce-scatter.4.cloned.1.call-update) | async-done | bytes 100368
  71.5 1.4 %copy.66 = f32[16,1568]{1,0:T(8,128)S(1)} copy(f32[16,1568]{0,1:T(8,128)} %bitcast.50) | data formatting | bytes 200704
  72.9 0.1 select_bitcast_fusion.1
  73.1 6.2 %all-gather = f32[4,1568,16]{1,2,0:T(8,128)S(1)} all-gather(f32[1,1568,16]{1,2,0:T(8,128)S(1)} %select_bitcast_fusion.1), channel_id=1, replica_groups=mesh['dp'=4,'cell'=8] {'dp'}, dimensions={0}, use_global_device_ids=true | all-gather | bytes 501760 | tf_op jit(solution)/shard_map/all_gather | solution.py:108
  79.3 0.2 copy.64
  79.5 1.0 %reshape.102 = f32[6272,16]{0,1:T(8,128)} reshape(f32[4,1568,16]{1,0,2:T(4,128)S(1)} %copy.64) | data formatting | bytes 802816
  (46 shorter events, 1.3 us)
Async XLA Ops:
  6.5 1.4 %copy-start = (bf16[128,6272]{1,0:T(8,128)(2,1)S(1)}, bf16[128,6272]{1,0:T(8,128)(2,1)}, u32[]{:S(2)}) copy-start(bf16[128,6272]{1,0:T(8,128)(2,1)} %param.8) | copy-start | bytes 4816900
  6.5 65.0 %reduce-scatter.4.cloned.1.call-start = ((), (), s32[]{:S(2)}) async-start(), calls=%async_computation.1 | async-start | bytes 4014080
  35.7 0.7 copy-start.4
  35.7 0.9 %copy-start.1 = (bf16[16,6272]{1,0:T(8,128)(2,1)S(1)}, bf16[16,6272]{1,0:T(8,128)(2,1)}, u32[]{:S(2)}) copy-start(bf16[16,6272]{1,0:T(8,128)(2,1)} %param.9) | copy-start | bytes 602116
  36.8 2.4 %copy-start.5 = (s32[1,2,128]{2,1,0:T(2,128)S(1)}, s32[1,2,128]{2,1,0:T(2,128)}, u32[]{:S(2)}) copy-start(s32[1,2,128]{2,1,0:T(2,128)} %param.12) | copy-start | bytes 3076
  42.9 7.9 %collective-permute-start.1 = (f32[17,128]{0,1:T(8,128)}, f32[17,128]{0,1:T(8,128)}, u32[]{:S(2)}, u32[]{:S(2)}) collective-permute-start(f32[17,128]{0,1:T(8,128)} %get-tuple-element.44), channel_id=1, source_target_pairs={{1,0},{2,1},{3,2},{4,3},{5,4},{6,5},{7,6},{9,8},{10,9},{11,10},{12... | collective-permute-start | bytes 26120 | tf_op jit(solution)/shard_map/ppermute | solution.py:15
  44.1 7.5 %collective-permute-start = (f32[17,128]{0,1:T(8,128)}, f32[17,128]{0,1:T(8,128)S(1)}, u32[]{:S(2)}, u32[]{:S(2)}) collective-permute-start(f32[17,128]{0,1:T(8,128)} %get-tuple-element.43), channel_id=1, source_target_pairs={{0,1},{1,2},{2,3},{3,4},{4,5},{5,6},{6,7},{8,9},{9,10},{10,11},{11... | collective-permute-start | bytes 26120 | tf_op jit(solution)/shard_map/ppermute | solution.py:14
  52.2 2.0 %copy-start.2 = (f32[2,7,17,112]{3,2,1,0:T(8,128)S(1)}, f32[2,7,17,112]{3,2,1,0:T(8,128)}, u32[]{:S(2)}) copy-start(f32[2,7,17,112]{3,2,1,0:T(8,128)} %get-tuple-element.76) | copy-start | bytes 319876 | tf_op jit(solution)/shard_map/while
  56.3 0.7 copy-start.3
  57.0 2.0 %copy-start.2 = (f32[2,7,17,112]{3,2,1,0:T(8,128)S(1)}, f32[2,7,17,112]{3,2,1,0:T(8,128)}, u32[]{:S(2)}) copy-start(f32[2,7,17,112]{3,2,1,0:T(8,128)} %get-tuple-element.76) | copy-start | bytes 319876 | tf_op jit(solution)/shard_map/while
  61.0 0.7 copy-start.3
Sparse Core Ops, SparseCore 0:
  35.9 35.6 reduce-scatter.3
where the time goes:
time: 87.7 us; the launch traced here: 87.3 us
  blocking collectives  29.6 us (34%)
  local copies, waits for them, and re-layouts  17 us (19%)
  between operations  14.4 us (16%)
  waiting for transfers between devices  8.71 us (10%)
  matrix products  5.93 us (7%)
  starting transfers between devices  5.83 us (7%)
  other arithmetic  5.74 us (7%)
    psum x1, blocking collectives, on_device(): summed = lax.psum(partial_data, 'cell')  23.4 us
    unnamed x2, waiting for transfers between devices  8.71 us
    unnamed x11, local copies, waits for them, and re-layouts  6.43 us
    all_gather x1, blocking collectives, on_device(): return lax.all_gather(total, 'dp', axis=1, tiled=True)  6.24 us
    ppermute x1, starting transfers between devices, padded_2(): before = lax.ppermute(last, axis, up)  4.55 us
    dot_general x2, matrix products, gather_block(): jnp.einsum('grw,gwb->grb', window_set, hits, precision=lax.Precision.HIGH...  4.16 us
    reduce_sum x2, other arithmetic, gather_block(): jnp.sum((column_set[:, :, None, :] == target).astype(jnp.float32), axis=1)  3.88 us
    gather x1, local copies, waits for them, and re-layouts, smoothness(): picked = jnp.take(values, send_lists[0].reshape(-1), axis=1)  2.89 us
  transfers between devices with their start and end apart: 3, of which 1 were waited for; matrix products, arithmetic and copies ran while one was open for 21% of the time, Pallas kernels for 0%

commit v1 on v0

v1 whole, which is shorter than its diff:
```python
import functools

import jax
import jax.numpy as jnp
from jax import lax
from jax.experimental import pallas as pl
from jax.experimental.pallas import tpu as pltpu
from jax.sharding import PartitionSpec as P

LANES = 128
REACH = 64
MESH = pl.DeviceIdType.MESH
F32 = jnp.float32
BF16 = jnp.bfloat16


def pick_chunk(blocks):
    for size in (5, 6, 4, 3, 2):
        if blocks % size == 0:
            return size
    return 1


def split2(value):
    hi = value.astype(BF16)
    return hi, (value - hi.astype(F32)).astype(BF16)


def stack_rows(weighted, weight):
    hi, lo = split2(weighted)
    w_hi, w_lo = split2(weight)
    shape = (16, weight.shape[1])
    row = lax.broadcasted_iota(jnp.int32, shape, 0)
    wide_hi = jnp.broadcast_to(w_hi.astype(F32), shape)
    wide_lo = jnp.broadcast_to(w_lo.astype(F32), shape)
    tail = jnp.where(row == 0, wide_hi, jnp.where(row == 1, wide_lo, F32(0.0)))
    return jnp.concatenate([hi, lo, tail.astype(BF16)], axis=0)


def count_hits(columns, rows):
    target = lax.broadcasted_iota(jnp.int32, (rows, columns.shape[1]), 0)
    hits = jnp.zeros((rows, columns.shape[1]), F32)
    for k in range(columns.shape[0]):
        hits = hits + jnp.where(columns[k : k + 1, :] == target, F32(1.0), F32(0.0))
    return hits.astype(BF16)


def kernel(
    n, n_dp, sens_hbm, dir_hbm, w_ref, cnt_ref, send_ref, nbr_hbm, out_ref,
    s_v, d_v, n_v, g, pmf, wrow, preds, rim_out, rim_in, acc, sm, ms, rs, ys,
    in_sem, bar_pred_s, bar_pred_r, rim_s, rim_r, rs_s, rs_r, y_s, y_r, fin_s, fin_r,
):
    nvec, slots = d_v.shape
    nb = slots // LANES
    half = (nb + 1) // 2
    swap_end = nb - half
    chunk = pick_chunk(half)
    n_chunks = half // chunk
    n_y = n_dp // 2
    piece = (half + n_y - 1) // n_y
    rim = rim_out.shape[2]

    cell = lax.axis_index("cell")
    dp = lax.axis_index("dp")
    y = dp // 2
    core = dp % 2
    sibling = y * 2 + 1 - core

    c_s = pltpu.make_async_copy(sens_hbm, s_v, in_sem.at[0])
    c_d = pltpu.make_async_copy(dir_hbm, d_v, in_sem.at[1])
    c_n = pltpu.make_async_copy(nbr_hbm, n_v, in_sem.at[2])
    c_d.start()
    c_s.start()
    c_n.start()

    barrier = pltpu.get_barrier_semaphore()
    for k in range(1, n):
        pl.semaphore_signal(barrier, inc=1, device_id={"cell": (cell + k) % n}, device_id_type=MESH)
    pl.semaphore_signal(barrier, inc=1, device_id={"dp": sibling}, device_id_type=MESH)
    for k in range(1, n_y):
        pl.semaphore_signal(
            barrier, inc=1, device_id={"dp": ((y + k) % n_y) * 2 + core}, device_id_type=MESH
        )

    count = cnt_ref[0]
    live = lax.broadcasted_iota(jnp.int32, (1, slots), 1) < count
    c_d.wait()
    masked = jnp.where(live, d_v[...].astype(F32), F32(0.0))
    pmf[...] = masked
    weight = jnp.where(live, w_ref[...], F32(0.0))
    wrow[...] = weight
    c_s.wait()
    preds[cell] = lax.dot_general(
        masked.astype(BF16), s_v[...], (((1,), (1,)), ((), ())), preferred_element_type=F32
    )

    pl.semaphore_wait(barrier, n + n_y - 1)
    sends = []
    for k in range(1, n):
        copy = pltpu.make_async_remote_copy(
            src_ref=preds.at[cell], dst_ref=preds.at[cell],
            send_sem=bar_pred_s.at[k], recv_sem=bar_pred_r.at[cell],
            device_id={"cell": (cell + k) % n}, device_id_type=MESH,
        )
        copy.start()
        sends.append(copy)

    pad = jnp.zeros((nvec, LANES), F32)
    wide = jnp.concatenate([masked * weight, pad], axis=1)
    wide_w = jnp.concatenate([weight, pad[:1]], axis=1)
    wide_w = pltpu.roll(jnp.broadcast_to(wide_w, (8, slots + LANES)), REACH, 1)
    g[...] = stack_rows(pltpu.roll(wide, REACH, 1), wide_w[0:1])

    lists = jnp.concatenate([send_ref[0, 0:1, :], send_ref[0, 1:2, :]], axis=1) + REACH
    step = 10 * LANES if (slots + LANES) % (10 * LANES) == 0 else LANES

    def pick(i, total):
        at = pl.multiple_of(i * step, step)
        hits = count_hits(lists - at, step)
        return total + jnp.dot(g[:, pl.ds(at, step)], hits, preferred_element_type=F32)

    picked = lax.fori_loop(
        0, (slots + LANES) // step, pick, jnp.zeros((3 * nvec, 2 * rim), F32)
    )
    for side in range(2):
        part = picked[:, side * rim : (side + 1) * rim]
        rim_out[side, 0:16] = part[0:16] + part[16:32]
        rim_out[side, 16:24] = jnp.broadcast_to(part[32:33] + part[33:34], (8, rim))
    for side in range(2):
        copy = pltpu.make_async_remote_copy(
            src_ref=rim_out.at[side], dst_ref=rim_in.at[1 - side],
            send_sem=rim_s.at[side], recv_sem=rim_r.at[1 - side],
            device_id={"cell": (cell + n - 1 + 2 * side) % n}, device_id_type=MESH,
        )
        copy.start()
        sends.append(copy)

    first_t = jnp.minimum(y * piece, half - piece)
    first_block = first_t + core * (nb - 2 * first_t - piece)
    sm[...] = jnp.zeros_like(sm)
    c_n.wait()

    def near(i, carry):
        at = pl.multiple_of((first_block + i) * LANES, LANES)
        hits = count_hits(n_v[:, pl.ds(at, LANES)] - at + REACH, 2 * LANES)
        acc[i] = jnp.dot(g[:, pl.ds(at, 2 * LANES)], hits, preferred_element_type=F32)
        return carry

    lax.fori_loop(0, piece, near, 0)

    sides = []
    for side in range(2):
        pltpu.make_async_remote_copy(
            src_ref=rim_out.at[side], dst_ref=rim_in.at[side],
            send_sem=rim_s.at[side], recv_sem=rim_r.at[side],
            device_id={"cell": (cell + n - 1 + 2 * side) % n}, device_id_type=MESH,
        ).wait_recv()
        there = cell > 0 if side == 0 else cell < n - 1
        got = jnp.where(there, rim_in[side], F32(0.0))
        sides.append(stack_rows(got[0:16], got[16:17]))
    rim_rows = jnp.concatenate(sides, axis=1)

    def far(i, carry):
        block = first_block + i
        at = pl.multiple_of(block * LANES, LANES)
        hits = count_hits(n_v[:, pl.ds(at, LANES)] - slots, 2 * rim)
        found = acc[i] + jnp.dot(rim_rows, hits, preferred_element_type=F32)
        sum_pw = found[0:16] + found[16:32]
        sum_w = found[32:33] + found[33:34]
        own_p = pmf[:, pl.ds(at, LANES)]
        own_w = wrow[:, pl.ds(at, LANES)]
        smooth = own_w * own_w * own_p + own_w * (own_p * sum_w - sum_pw)
        t = block + core * (nb - 1 - 2 * block)
        mine = jnp.logical_and(t >= y * piece, t < (y + 1) * piece)
        sm[:, pl.ds(at, LANES)] = smooth * jnp.where(mine, F32(0.5), F32(0.0))
        return carry

    lax.fori_loop(0, piece, far, 0)

    for k in range(1, n):
        source = (cell + k) % n
        pltpu.make_async_remote_copy(
            src_ref=preds.at[source], dst_ref=preds.at[source],
            send_sem=bar_pred_s.at[k], recv_sem=bar_pred_r.at[source],
            device_id={"cell": source}, device_id_type=MESH,
        ).wait_recv()
    predicted = preds[0]
    for k in range(1, n):
        predicted = predicted + preds[k]
    stacked = jnp.concatenate(split2(predicted), axis=0)

    def misfit(at):
        both = jnp.dot(stacked, s_v[:, pl.ds(at, chunk * LANES)], preferred_element_type=F32)
        return both[:nvec] + both[nvec:]

    def lanes_at(block):
        return pl.multiple_of(block * LANES, LANES)

    for c in range(n_chunks):
        a, b = c * chunk, (c + 1) * chunk
        ms[c] = misfit(lanes_at((1 - core) * (nb - b) + core * a))
        copy = pltpu.make_async_remote_copy(
            src_ref=ms.at[c], dst_ref=rs.at[c], send_sem=rs_s.at[c], recv_sem=rs_r.at[c],
            device_id={"dp": sibling}, device_id_type=MESH,
        )
        copy.start()
        sends.append(copy)

    for c in range(n_chunks):
        a, b = c * chunk, (c + 1) * chunk
        at = lanes_at(core * (nb - b) + (1 - core) * a)
        own = misfit(at)
        pltpu.make_async_remote_copy(
            src_ref=ms.at[c], dst_ref=rs.at[c], send_sem=rs_s.at[c], recv_sem=rs_r.at[c],
            device_id={"dp": sibling}, device_id_type=MESH,
        ).wait_recv()
        ys[y, c] = (own + rs[c]) + sm[:, pl.ds(at, chunk * LANES)]
        for k in range(1, n_y):
            copy = pltpu.make_async_remote_copy(
                src_ref=ys.at[y, c], dst_ref=ys.at[y, c],
                send_sem=y_s.at[k, c], recv_sem=y_r.at[y, c],
                device_id={"dp": ((y + k) % n_y) * 2 + core}, device_id_type=MESH,
            )
            copy.start()
            sends.append(copy)

    final = []
    for c in range(n_chunks):
        a, b = c * chunk, (c + 1) * chunk
        at = lanes_at(core * (nb - b) + (1 - core) * a)
        for k in range(1, n_y):
            source = (y + k) % n_y
            pltpu.make_async_remote_copy(
                src_ref=ys.at[source, c], dst_ref=ys.at[source, c],
                send_sem=y_s.at[k, c], recv_sem=y_r.at[source, c],
                device_id={"dp": source * 2 + core}, device_id_type=MESH,
            ).wait_recv()
        total = ys[0, c]
        for k in range(1, n_y):
            total = total + ys[k, c]
        place = lax.broadcasted_iota(jnp.int32, (1, chunk * LANES), 1) + at
        out_ref[:, pl.ds(at, chunk * LANES)] = jnp.where(place < count, total, F32(0.0))
        end = min(b, swap_end)
        if end > a:
            width = (end - a) * LANES
            here = lanes_at(core * (nb - end) + (1 - core) * a)
            there = lanes_at((1 - core) * (nb - end) + core * a)
            copy = pltpu.make_async_remote_copy(
                src_ref=out_ref.at[:, pl.ds(here, width)], dst_ref=out_ref.at[:, pl.ds(here, width)],
                send_sem=fin_s.at[c], recv_sem=fin_r.at[c],
                device_id={"dp": sibling}, device_id_type=MESH,
            )
            copy.start()
            sends.append(copy)
            final.append(
                pltpu.make_async_remote_copy(
                    src_ref=out_ref.at[:, pl.ds(there, width)],
                    dst_ref=out_ref.at[:, pl.ds(there, width)],
                    send_sem=fin_s.at[c], recv_sem=fin_r.at[c],
                    device_id={"dp": sibling}, device_id_type=MESH,
                )
            )
    for copy in final:
        copy.wait_recv()
    for copy in sends:
        copy.wait_send()


def on_device(n, n_dp, sensitivity, direction, depth_weight, counts, send_lists, neighbours):
    ndata, slots = sensitivity.shape
    nvec = direction.shape[0]
    faces = neighbours.shape[0]
    rim = send_lists.shape[2]
    nb = slots // LANES
    half = (nb + 1) // 2
    chunk = pick_chunk(half)
    n_chunks = half // chunk
    n_y = n_dp // 2
    piece = (half + n_y - 1) // n_y
    vmem = pl.BlockSpec(memory_space=pltpu.VMEM)
    hbm = pl.BlockSpec(memory_space=pl.ANY)
    dma = pltpu.SemaphoreType.DMA
    return pl.pallas_call(
        functools.partial(kernel, n, n_dp),
        out_shape=jax.ShapeDtypeStruct((nvec, slots), F32),
        in_specs=[hbm, hbm, vmem, pl.BlockSpec(memory_space=pltpu.SMEM), vmem, hbm],
        out_specs=vmem,
        scratch_shapes=[
            pltpu.VMEM((ndata, slots), BF16),
            pltpu.VMEM((nvec, slots), BF16),
            pltpu.VMEM((faces, slots), jnp.int32),
            pltpu.VMEM((3 * nvec, slots + LANES), BF16),
            pltpu.VMEM((nvec, slots), F32),
            pltpu.VMEM((1, slots), F32),
            pltpu.VMEM((n, nvec, ndata), F32),
            pltpu.VMEM((2, nvec + 8, rim), F32),
            pltpu.VMEM((2, nvec + 8, rim), F32),
            pltpu.VMEM((piece, 3 * nvec, LANES), F32),
            pltpu.VMEM((nvec, slots), F32),
            pltpu.VMEM((n_chunks, nvec, chunk * LANES), F32),
            pltpu.VMEM((n_chunks, nvec, chunk * LANES), F32),
            pltpu.VMEM((n_y, n_chunks, nvec, chunk * LANES), F32),
            dma((3,)),
            dma((n,)),
            dma((n,)),
            dma((2,)),
            dma((2,)),
            dma((n_chunks,)),
            dma((n_chunks,)),
            dma((n_y, n_chunks)),
            dma((n_y, n_chunks)),
            dma((n_chunks,)),
            dma((n_chunks,)),
        ],
        compiler_params=pltpu.CompilerParams(
            collective_id=0, has_side_effects=True, vmem_limit_bytes=40 * 1024 * 1024
        ),
    )(sensitivity, direction, depth_weight.reshape(1, slots), counts, send_lists, neighbours)


def solution(mesh):
    placed = (
        P("dp", "cell"),
        P(None, "cell"),
        P("cell"),
        P("cell"),
        P("cell", None, None),
        P(None, "cell"),
    )
    return jax.shard_map(
        functools.partial(on_device, mesh.shape["cell"], mesh.shape["dp"]),
        mesh=mesh, in_specs=placed, out_specs=P(None, "cell"), check_vma=False,
    )
```

time: 87.7 us -> 29.8 us (0.34)
  blocking collectives: 29.6 us -> 0 us
  Pallas kernels: 0 us -> 23.4 us
  between operations: 14.4 us -> 0.68 us
  local copies, waits for them, and re-layouts: 17 us -> 5.47 us
  waiting for transfers between devices: 8.71 us -> 0 us
  matrix products: 5.93 us -> 0 us
  starting transfers between devices: 5.83 us -> 0 us
  other arithmetic: 5.74 us -> 0 us
    psum x1 -> x0, blocking collectives: 23.4 us -> none  [on_device(): summed = lax.psum(partial_data, 'cell')]
    pallas_call x0 -> x1, Pallas kernels: none -> 23.4 us  [on_device(): pl.pallas_call(functools.partial(kernel, n, n_dp), out_shape=jax.ShapeDty...]
    unnamed x2 -> x0, waiting for transfers between devices: 8.71 us -> none
    all_gather x1 -> x0, blocking collectives: 6.24 us -> none  [on_device(): return lax.all_gather(total, 'dp', axis=1, tiled=True)]
    dot_general x4 -> x0, matrix products: 5.93 us -> none  [the longest x2 4.16 us: gather_block(): jnp.einsum('grw,gwb->grb', window_set, hits, precision=lax.Precision.HIGH...]
    ppermute x2 -> x0, starting transfers between devices: 5.83 us -> none  [the longest x1 4.55 us: padded_2(): before = lax.ppermute(last, axis, up)]
    reduce_sum x2 -> x0, other arithmetic: 3.88 us -> none  [gather_block(): jnp.sum((column_set[:, :, None, :] == target).astype(jnp.float32), axis=1)]
    gather x1 -> x0, local copies, waits for them, and re-layouts: 2.89 us -> none  [smoothness(): picked = jnp.take(values, send_lists[0].reshape(-1), axis=1)]
  transfers between devices with their start and end apart: 3 -> 0, of which waited for: 1 -> 0; matrix products, arithmetic and copies ran while one was open for 21% -> 0% of each run, Pallas kernels for 0% -> 0%
where the time goes in v1:
time: 29.8 us; the launch traced here: 29.5 us
  Pallas kernels  23.4 us (79%)
  local copies, waits for them, and re-layouts  5.47 us (18%)
  between operations  0.68 us (2%)
    pallas_call x1, Pallas kernels, on_device(): pl.pallas_call(functools.partial(kernel, n, n_dp), out_shape=jax.ShapeDty...  23.4 us
    unnamed x9, local copies, waits for them, and re-layouts  4.7 us
    reshape x1, local copies, waits for them, and re-layouts, on_device(): depth_weight.reshape(1, slots)  0.77 us

profile of v1, /device:TPU:0, one launch (start us, length us, event | category | flops | bytes accessed | tf_op | source)
XLA Modules:
  0.0 29.5 jit_solution(12071375638842181699)
XLA Ops:
  0.7 0.8 %reshape.3.w_ref = f32[1,6272]{1,0:T(1,128)S(1)} reshape(f32[6272]{0:T(1024)} %param.8) | data formatting | bytes 50176 | tf_op jit(solution)/shard_map/reshape | solution.py:318
  1.4 0.0 copy-start
  1.4 1.4 %copy-done = bf16[128,6272]{1,0:T(8,128)(2,1)S(1)} copy-done((bf16[128,6272]{1,0:T(8,128)(2,1)S(1)}, bf16[128,6272]{1,0:T(8,128)(2,1)}, u32[]{:S(2)}) %copy-start) | copy-done | bytes 1605656
  2.8 0.0 copy-start.1
  2.8 0.9 %copy-done.1 = bf16[16,6272]{1,0:T(8,128)(2,1)S(1)} copy-done((bf16[16,6272]{1,0:T(8,128)(2,1)S(1)}, bf16[16,6272]{1,0:T(8,128)(2,1)}, u32[]{:S(2)}) %copy-start.1) | copy-done | bytes 200728
  3.8 0.0 copy-start.2
  3.8 0.9 %copy-done.2 = s32[6,6272]{1,0:T(8,128)S(1)} copy-done((s32[6,6272]{1,0:T(8,128)S(1)}, s32[6,6272]{1,0:T(8,128)}, u32[]{:S(2)}) %copy-start.2) | copy-done | bytes 150552
  4.7 0.0 copy-start.3
  4.7 0.7 %copy-done.3 = s32[1,2,128]{2,1,0:T(2,128)S(1)} copy-done((s32[1,2,128]{2,1,0:T(2,128)S(1)}, s32[1,2,128]{2,1,0:T(2,128)}, u32[]{:S(2)}) %copy-start.3) | copy-done | bytes 1048
  5.4 23.4 %shard_map.64 = f32[16,6272]{1,0:T(8,128)S(1)} custom-call(bf16[128,6272]{1,0:T(8,128)(2,1)S(1)} %copy-done, bf16[16,6272]{1,0:T(8,128)(2,1)S(1)} %copy-done.1, f32[1,6272]{1,0:T(1,128)S(1)} %reshape.3.w_ref, s32[1]{0:T(128)S(6)} %copy.8.cnt_ref, s32[1,2,128]{2,1,0:T(2,128)S(1)} %copy-done.3, s32[6,6272]{1,0:T(8,128)S(1)} %copy-done.2), custom_call_target="tpu_custom_call" | custom-call | tf_op jit(solution)/shard_map/pallas_call | solution.py:283
  28.8 0.8 %copy.9 = f32[16,6272]{1,0:T(8,128)} copy(f32[16,6272]{1,0:T(8,128)S(1)} %shard_map.64) | data formatting | bytes 802816
Async XLA Ops:
  1.4 1.4 %copy-start = (bf16[128,6272]{1,0:T(8,128)(2,1)S(1)}, bf16[128,6272]{1,0:T(8,128)(2,1)}, u32[]{:S(2)}) copy-start(bf16[128,6272]{1,0:T(8,128)(2,1)} %sens_hbm.1) | copy-start | bytes 4816900
  2.8 0.9 %copy-start.1 = (bf16[16,6272]{1,0:T(8,128)(2,1)S(1)}, bf16[16,6272]{1,0:T(8,128)(2,1)}, u32[]{:S(2)}) copy-start(bf16[16,6272]{1,0:T(8,128)(2,1)} %dir_hbm.1) | copy-start | bytes 602116
  3.8 0.9 %copy-start.2 = (s32[6,6272]{1,0:T(8,128)S(1)}, s32[6,6272]{1,0:T(8,128)}, u32[]{:S(2)}) copy-start(s32[6,6272]{1,0:T(8,128)} %nbr_hbm.1) | copy-start | bytes 451588
  4.7 0.7 %copy-start.3 = (s32[1,2,128]{2,1,0:T(2,128)S(1)}, s32[1,2,128]{2,1,0:T(2,128)}, u32[]{:S(2)}) copy-start(s32[1,2,128]{2,1,0:T(2,128)} %send_ref.1) | copy-start | bytes 3076

commit v2 on v1

--- a/solution.py
+++ b/solution.py
@@ -38,16 +38,17 @@
 
 
 def count_hits(columns, rows):
-    target = lax.broadcasted_iota(jnp.int32, (rows, columns.shape[1]), 0)
-    hits = jnp.zeros((rows, columns.shape[1]), F32)
+    narrow = columns.astype(jnp.int16)
+    target = lax.broadcasted_iota(jnp.int16, (rows, columns.shape[1]), 0)
+    hits = jnp.zeros((rows, columns.shape[1]), BF16)
     for k in range(columns.shape[0]):
-        hits = hits + jnp.where(columns[k : k + 1, :] == target, F32(1.0), F32(0.0))
-    return hits.astype(BF16)
+        hits = hits + jnp.where(narrow[k : k + 1, :] == target, BF16(1.0), BF16(0.0))
+    return hits
 
 
 def kernel(
-    n, n_dp, sens_hbm, dir_hbm, w_ref, cnt_ref, send_ref, nbr_hbm, out_ref,
-    s_v, d_v, n_v, g, pmf, wrow, preds, rim_out, rim_in, acc, sm, ms, rs, ys,
+    n, n_dp, sens_hbm, dir_hbm, w_hbm, cnt_ref, send_hbm, nbr_hbm, out_ref,
+    s_v, d_v, n_v, w_v, l_v, g, pmf, wrow, preds, rim_out, rim_in, acc, sm, ms, rs, ys,
     in_sem, bar_pred_s, bar_pred_r, rim_s, rim_r, rs_s, rs_r, y_s, y_r, fin_s, fin_r,
 ):
     nvec, slots = d_v.shape
@@ -69,8 +70,12 @@
     c_s = pltpu.make_async_copy(sens_hbm, s_v, in_sem.at[0])
     c_d = pltpu.make_async_copy(dir_hbm, d_v, in_sem.at[1])
     c_n = pltpu.make_async_copy(nbr_hbm, n_v, in_sem.at[2])
+    c_w = pltpu.make_async_copy(w_hbm, w_v, in_sem.at[3])
+    c_l = pltpu.make_async_copy(send_hbm, l_v, in_sem.at[4])
     c_d.start()
     c_s.start()
+    c_w.start()
+    c_l.start()
     c_n.start()
 
     barrier = pltpu.get_barrier_semaphore()
@@ -87,8 +92,6 @@
     c_d.wait()
     masked = jnp.where(live, d_v[...].astype(F32), F32(0.0))
     pmf[...] = masked
-    weight = jnp.where(live, w_ref[...], F32(0.0))
-    wrow[...] = weight
     c_s.wait()
     preds[cell] = lax.dot_general(
         masked.astype(BF16), s_v[...], (((1,), (1,)), ((), ())), preferred_element_type=F32
@@ -105,13 +108,20 @@
         copy.start()
         sends.append(copy)
 
+    c_w.wait()
+    for j in range(nb):
+        wrow[:, j * LANES : (j + 1) * LANES] = w_v[j : j + 1, :]
+    weight = jnp.where(live, wrow[...], F32(0.0))
+    wrow[...] = weight
+
     pad = jnp.zeros((nvec, LANES), F32)
     wide = jnp.concatenate([masked * weight, pad], axis=1)
     wide_w = jnp.concatenate([weight, pad[:1]], axis=1)
     wide_w = pltpu.roll(jnp.broadcast_to(wide_w, (8, slots + LANES)), REACH, 1)
     g[...] = stack_rows(pltpu.roll(wide, REACH, 1), wide_w[0:1])
 
-    lists = jnp.concatenate([send_ref[0, 0:1, :], send_ref[0, 1:2, :]], axis=1) + REACH
+    c_l.wait()
+    lists = jnp.concatenate([l_v[0, 0:1, :], l_v[0, 1:2, :]], axis=1) + REACH
     step = 10 * LANES if (slots + LANES) % (10 * LANES) == 0 else LANES
 
     def pick(i, total):
@@ -146,7 +156,7 @@
         acc[i] = jnp.dot(g[:, pl.ds(at, 2 * LANES)], hits, preferred_element_type=F32)
         return carry
 
-    lax.fori_loop(0, piece, near, 0)
+    lax.fori_loop(0, piece, near, 0, unroll=True)
 
     sides = []
     for side in range(2):
@@ -175,7 +185,7 @@
         sm[:, pl.ds(at, LANES)] = smooth * jnp.where(mine, F32(0.5), F32(0.0))
         return carry
 
-    lax.fori_loop(0, piece, far, 0)
+    lax.fori_loop(0, piece, far, 0, unroll=True)
 
     for k in range(1, n):
         source = (cell + k) % n
@@ -278,17 +288,19 @@
     n_y = n_dp // 2
     piece = (half + n_y - 1) // n_y
     vmem = pl.BlockSpec(memory_space=pltpu.VMEM)
-    hbm = pl.BlockSpec(memory_space=pl.ANY)
+    hbm = pl.BlockSpec(memory_space=pltpu.HBM)
     dma = pltpu.SemaphoreType.DMA
     return pl.pallas_call(
         functools.partial(kernel, n, n_dp),
         out_shape=jax.ShapeDtypeStruct((nvec, slots), F32),
-        in_specs=[hbm, hbm, vmem, pl.BlockSpec(memory_space=pltpu.SMEM), vmem, hbm],
+        in_specs=[hbm, hbm, hbm, pl.BlockSpec(memory_space=pltpu.SMEM), hbm, hbm],
         out_specs=vmem,
         scratch_shapes=[
             pltpu.VMEM((ndata, slots), BF16),
             pltpu.VMEM((nvec, slots), BF16),
             pltpu.VMEM((faces, slots), jnp.int32),
+            pltpu.VMEM((nb, LANES), F32),
+            pltpu.VMEM(send_lists.shape, jnp.int32),
             pltpu.VMEM((3 * nvec, slots + LANES), BF16),
             pltpu.VMEM((nvec, slots), F32),
             pltpu.VMEM((1, slots), F32),
@@ -300,7 +312,7 @@
             pltpu.VMEM((n_chunks, nvec, chunk * LANES), F32),
             pltpu.VMEM((n_chunks, nvec, chunk * LANES), F32),
             pltpu.VMEM((n_y, n_chunks, nvec, chunk * LANES), F32),
-            dma((3,)),
+            dma((5,)),
             dma((n,)),
             dma((n,)),
             dma((2,)),
@@ -313,9 +325,9 @@
             dma((n_chunks,)),
         ],
         compiler_params=pltpu.CompilerParams(
-            collective_id=0, has_side_effects=True, vmem_limit_bytes=40 * 1024 * 1024
+            collective_id=0, has_side_effects=True, vmem_limit_bytes=64000 * 1024
         ),
-    )(sensitivity, direction, depth_weight.reshape(1, slots), counts, send_lists, neighbours)
+    )(sensitivity, direction, depth_weight.reshape(nb, LANES), counts, send_lists, neighbours)
 
 
 def solution(mesh):

time: 29.8 us -> 24.9 us (0.84)
  local copies, waits for them, and re-layouts: 5.47 us -> 1.77 us
  Pallas kernels: 23.4 us -> 22.3 us
    unnamed x9 -> x1, local copies, waits for them, and re-layouts: 4.7 us -> 1.77 us
    pallas_call x1, Pallas kernels: 23.4 us -> 22.3 us  [on_device(): pl.pallas_call(functools.partial(kernel, n, n_dp), out_shape=jax.ShapeDty...]
    reshape x1 -> x0, local copies, waits for them, and re-layouts: 0.77 us -> none  [on_device(): depth_weight.reshape(1, slots)]
where the time goes in v2:
time: 24.9 us; the launch traced here: 24.8 us
  Pallas kernels  22.3 us (90%)
  local copies, waits for them, and re-layouts  1.77 us (7%)
  between operations  0.66 us (3%)
    pallas_call x1, Pallas kernels, on_device(): pl.pallas_call(functools.partial(kernel, n, n_dp), out_shape=jax.ShapeDty...  22.3 us
    unnamed x1, local copies, waits for them, and re-layouts  1.77 us

profile of v2, /device:TPU:0, one launch (start us, length us, event | category | flops | bytes accessed | tf_op | source)
XLA Modules:
  0.0 24.8 jit_solution(7633287471491260138)
XLA Ops:
  0.7 22.3 %shard_map.64 = f32[16,6272]{1,0:T(8,128)} custom-call(bf16[128,6272]{1,0:T(8,128)(2,1)} %sens_hbm.1, bf16[16,6272]{1,0:T(8,128)(2,1)} %dir_hbm.1, f32[49,128]{1,0:T(8,128)} %bitcast.1, s32[1]{0:T(128)S(6)} %copy.8.cnt_ref, s32[1,2,128]{2,1,0:T(2,128)} %send_hbm.1, s32[6,6272]{1,0:T(8,128)} %nbr_hbm.1), custom_call_target="tpu_custom_call" | custom-call | tf_op jit(solution)/shard_map/pallas_call | solution.py:293
  23.0 1.8 %copy.9 = f32[16,6272]{1,0:T(8,128)} copy(f32[16,6272]{1,0:T(8,128)} %shard_map.64) | data formatting | bytes 802816

commit v3 on v2

--- a/solution.py
+++ b/solution.py
@@ -130,7 +130,7 @@
         return total + jnp.dot(g[:, pl.ds(at, step)], hits, preferred_element_type=F32)
 
     picked = lax.fori_loop(
-        0, (slots + LANES) // step, pick, jnp.zeros((3 * nvec, 2 * rim), F32)
+        0, (slots + LANES) // step, pick, jnp.zeros((3 * nvec, 2 * rim), F32), unroll=True
     )
     for side in range(2):
         part = picked[:, side * rim : (side + 1) * rim]

time: 24.9 us -> 25 us (level)
  no operation moved by 1% of the time
where the time goes in v3:
time: 25 us; the launch traced here: 24.9 us
  Pallas kernels  22.4 us (90%)
  local copies, waits for them, and re-layouts  1.77 us (7%)
  between operations  0.66 us (3%)
    pallas_call x1, Pallas kernels, on_device(): pl.pallas_call(functools.partial(kernel, n, n_dp), out_shape=jax.ShapeDty...  22.4 us
    unnamed x1, local copies, waits for them, and re-layouts  1.77 us

profile of v3, /device:TPU:0, one launch (start us, length us, event | category | flops | bytes accessed | tf_op | source)
XLA Modules:
  0.0 24.9 jit_solution(4150106065292862053)
XLA Ops:
  0.7 22.4 %shard_map.64 = f32[16,6272]{1,0:T(8,128)} custom-call(bf16[128,6272]{1,0:T(8,128)(2,1)} %sens_hbm.1, bf16[16,6272]{1,0:T(8,128)(2,1)} %dir_hbm.1, f32[49,128]{1,0:T(8,128)} %bitcast.1, s32[1]{0:T(128)S(6)} %copy.8.cnt_ref, s32[1,2,128]{2,1,0:T(2,128)} %send_hbm.1, s32[6,6272]{1,0:T(8,128)} %nbr_hbm.1), custom_call_target="tpu_custom_call" | custom-call | tf_op jit(solution)/shard_map/pallas_call | solution.py:293
  23.1 1.8 %copy.9 = f32[16,6272]{1,0:T(8,128)} copy(f32[16,6272]{1,0:T(8,128)} %shard_map.64) | data formatting | bytes 802816

commit v4 on v2

--- a/solution.py
+++ b/solution.py
@@ -47,9 +47,9 @@
 
 
 def kernel(
-    n, n_dp, sens_hbm, dir_hbm, w_hbm, cnt_ref, send_hbm, nbr_hbm, out_ref,
+    n, n_dp, sens_hbm, dir_hbm, w_hbm, cnt_ref, send_hbm, nbr_hbm, out_hbm,
     s_v, d_v, n_v, w_v, l_v, g, pmf, wrow, preds, rim_out, rim_in, acc, sm, ms, rs, ys,
-    in_sem, bar_pred_s, bar_pred_r, rim_s, rim_r, rs_s, rs_r, y_s, y_r, fin_s, fin_r,
+    in_sem, bar_pred_s, bar_pred_r, rim_s, rim_r, rs_s, rs_r, y_s, y_r, fin_s, fin_r, out_ref, o_s,
 ):
     nvec, slots = d_v.shape
     nb = slots // LANES
@@ -234,7 +234,14 @@
             copy.start()
             sends.append(copy)
 
+    def write_back(block, width, slot):
+        part = pl.ds(lanes_at(block), width)
+        copy = pltpu.make_async_copy(out_ref.at[:, part], out_hbm.at[:, part], o_s.at[slot])
+        copy.start()
+        return copy
+
     final = []
+    writes = []
     for c in range(n_chunks):
         a, b = c * chunk, (c + 1) * chunk
         at = lanes_at(core * (nb - b) + (1 - core) * a)
@@ -250,6 +257,9 @@
             total = total + ys[k, c]
         place = lax.broadcasted_iota(jnp.int32, (1, chunk * LANES), 1) + at
         out_ref[:, pl.ds(at, chunk * LANES)] = jnp.where(place < count, total, F32(0.0))
+        writes.append(
+            write_back(core * (nb - b) + (1 - core) * a, chunk * LANES, c)
+        )
         end = min(b, swap_end)
         if end > a:
             width = (end - a) * LANES
@@ -262,16 +272,20 @@
             )
             copy.start()
             sends.append(copy)
-            final.append(
+            final.append((
+                (1 - core) * (nb - end) + core * a, width, n_chunks + c,
                 pltpu.make_async_remote_copy(
                     src_ref=out_ref.at[:, pl.ds(there, width)],
                     dst_ref=out_ref.at[:, pl.ds(there, width)],
                     send_sem=fin_s.at[c], recv_sem=fin_r.at[c],
                     device_id={"dp": sibling}, device_id_type=MESH,
-                )
-            )
-    for copy in final:
+                ),
+            ))
+    for block, width, slot, copy in final:
         copy.wait_recv()
+        writes.append(write_back(block, width, slot))
+    for copy in writes:
+        copy.wait()
     for copy in sends:
         copy.wait_send()
 
@@ -294,7 +308,7 @@
         functools.partial(kernel, n, n_dp),
         out_shape=jax.ShapeDtypeStruct((nvec, slots), F32),
         in_specs=[hbm, hbm, hbm, pl.BlockSpec(memory_space=pltpu.SMEM), hbm, hbm],
-        out_specs=vmem,
+        out_specs=hbm,
         scratch_shapes=[
             pltpu.VMEM((ndata, slots), BF16),
             pltpu.VMEM((nvec, slots), BF16),
@@ -323,6 +337,8 @@
             dma((n_y, n_chunks)),
             dma((n_chunks,)),
             dma((n_chunks,)),
+            pltpu.VMEM((nvec, slots), F32),
+            dma((2 * n_chunks,)),
         ],
         compiler_params=pltpu.CompilerParams(
             collective_id=0, has_side_effects=True, vmem_limit_bytes=64000 * 1024

time: 24.9 us -> 24.8 us (level)
  Pallas kernels: 22.3 us -> 22 us
    pallas_call x1, Pallas kernels: 22.3 us -> 22 us  [on_device(): pl.pallas_call(functools.partial(kernel, n, n_dp), out_shape=jax.ShapeDty...]
where the time goes in v4:
time: 24.8 us; the launch traced here: 24.4 us
  Pallas kernels  22 us (89%)
  local copies, waits for them, and re-layouts  1.77 us (7%)
  between operations  0.66 us (3%)
    pallas_call x1, Pallas kernels, on_device(): pl.pallas_call(functools.partial(kernel, n, n_dp), out_shape=jax.ShapeDty...  22 us
    unnamed x1, local copies, waits for them, and re-layouts  1.77 us

profile of v4, /device:TPU:0, one launch (start us, length us, event | category | flops | bytes accessed | tf_op | source)
XLA Modules:
  0.0 24.4 jit_solution(13066194096556024369)
XLA Ops:
  0.7 22.0 %shard_map.64 = f32[16,6272]{1,0:T(8,128)} custom-call(bf16[128,6272]{1,0:T(8,128)(2,1)} %sens_hbm.1, bf16[16,6272]{1,0:T(8,128)(2,1)} %dir_hbm.1, f32[49,128]{1,0:T(8,128)} %bitcast.1, s32[1]{0:T(128)S(6)} %copy.8.cnt_ref, s32[1,2,128]{2,1,0:T(2,128)} %send_hbm.1, s32[6,6272]{1,0:T(8,128)} %nbr_hbm.1), custom_call_target="tpu_custom_call" | custom-call | tf_op jit(solution)/shard_map/pallas_call | solution.py:307
  22.6 1.8 %copy.9 = f32[16,6272]{1,0:T(8,128)} copy(f32[16,6272]{1,0:T(8,128)} %shard_map.64) | data formatting | bytes 802816
